TPU v7x, 128 devices: a whole 4x4x4 slice. The times are simulated.
128 devices in a mesh: row: 8 (over z, x_lo), col: 16 (over x_hi, y, core).
Axes of the slice: x: 4 (x_hi: 2, x_lo: 2; x = x_hi * 2 + x_lo), y: 4, z: 4, core: 2. Of those that a mesh axis runs over, the one named last changes fastest.
Arguments:
- front: float32 [45056, 4096], P('row', 'col'), may hold values from -6 to 278, as said below
- children: float32 [32768, 4096], P('row', 'col'), may hold values from -6 to 6
- row_map: int32 [256], replicated, may hold values from 0 to 351, as said below
- col_map: int32 [64], replicated, may hold values from 0 to 31, as said below
Outputs:
- updated: float32 [45056, 4096], P('row', 'col')
Inputs may be any that keep to these rules, and one draw needn't show every extreme that they name: `front`: the symmetric part of the assembled leading 512 x 512 block is positive definite. `row_map`: within one child no front row block is named twice. Of the 32 child row blocks stored on one device, at most 8 name front row blocks of one owner (block index modulo 8); one owner, the same for every device, is named exactly 8 times by every device. Within one child no front column block is named twice, and col_map[h * 32 + b] modulo 16 equals b // 2.
All inputs are finite; a program needn't handle non-finite values.
Results may differ from a plain program's by a relative error of at most 0.00005.
Values sent between devices are 32-bit elements; how exact they have to be, the bound alone decides.
A program may use at most 128 MiB of HBM per device.

v0:
```python
import jax
import jax.numpy as jnp
from jax import lax
from jax.sharding import PartitionSpec as P

BLK = 128
PANEL = 512


def broadcast(x, axis, root):
    mine = lax.axis_index(axis) == root
    return lax.psum(jnp.where(mine, x, jnp.zeros_like(x)), axis)


def factor_rows(panel_rows, lower_factor):
    return jax.scipy.linalg.solve_triangular(lower_factor, panel_rows.T, lower=True).T


def local(front, children, row_map, col_map):
    row_count = lax.axis_size("row")
    col_count = lax.axis_size("col")
    my_row = lax.axis_index("row")
    my_col = lax.axis_index("col")
    local_rows = front.shape[0] // BLK
    local_cols = front.shape[1] // BLK
    child_rows = children.shape[0] // BLK
    child_cols = children.shape[1] // BLK
    halfway = row_count // 2
    capacity = 2 * child_rows // row_count
    slot_count = row_count * capacity
    layout = row_map.reshape(row_count, child_rows)
    owner_rows = layout % row_count
    local_place = layout // row_count
    counter = jnp.arange(child_rows)
    earlier = (owner_rows[:, :, None] == owner_rows[:, None, :]) & (
        counter[None, None, :] < counter[None, :, None]
    )
    rank_index = jnp.sum(earlier.astype(jnp.int32), axis=2)
    slot_index = owner_rows * capacity + rank_index
    my_slots = lax.dynamic_index_in_dim(slot_index, my_row, 0, keepdims=False)
    picker = (jnp.arange(slot_count)[:, None] == my_slots[None, :]).astype(jnp.float32)
    flat_rows = children.reshape(child_rows, BLK * child_cols * BLK)
    outgoing = jnp.dot(picker, flat_rows, precision=lax.Precision.HIGHEST).reshape(
        row_count, capacity, BLK * child_cols * BLK
    )
    incoming = lax.all_to_all(outgoing, "row", split_axis=0, concat_axis=0, tiled=True)
    is_mine = owner_rows == my_row
    slot_of = jnp.where(is_mine, rank_index, -1)
    slot_hit = (slot_of[:, :, None] == jnp.arange(capacity)[None, None, :]).astype(jnp.float32)
    target = (local_place[:, :, None] == jnp.arange(local_rows)[None, None, :]).astype(jnp.float32)
    row_route = jnp.einsum(
        "sum,suk->ksm", slot_hit, target, precision=lax.Precision.HIGHEST
    ).reshape(local_rows, slot_count)
    column_maps = col_map.reshape(2, col_count, child_cols)
    my_columns = lax.dynamic_index_in_dim(column_maps, my_col, 1, keepdims=False) // col_count
    source_columns = my_columns[jnp.arange(row_count) // halfway]
    column_pick = (source_columns[:, :, None] == jnp.arange(local_cols)[None, None, :]).astype(
        jnp.float32
    )
    received = incoming.reshape(row_count, capacity, BLK, child_cols, BLK)
    placed = jnp.einsum("stq,smitj->smiqj", column_pick, received, precision=lax.Precision.HIGHEST)
    placed = placed.reshape(slot_count, BLK * local_cols * BLK)
    added_tiles = jnp.dot(row_route, placed, precision=lax.Precision.HIGHEST).reshape(
        local_rows * BLK, local_cols * BLK
    )
    assembled = front + added_tiles
    panel_blocks = PANEL // BLK
    own_block = assembled[:, :BLK]
    pieces = []
    for source in range(panel_blocks):
        pieces.append(broadcast(own_block, "col", source))
    panel_block = jnp.concatenate(pieces, axis=1)
    leading = lax.all_gather(panel_block[:BLK], "row", axis=0, tiled=True)[:PANEL]
    lower_factor = jnp.linalg.cholesky((leading + leading.T) * 0.5)
    factor = factor_rows(panel_block, lower_factor)
    lead_rows = lax.dynamic_slice_in_dim(
        lower_factor, jnp.minimum(my_row, panel_blocks - 1) * BLK, BLK, 0
    )
    first_rows = jnp.where(my_row < panel_blocks, lead_rows, factor[:BLK])
    factor = jnp.concatenate([first_rows, factor[BLK:]], axis=0)
    stride = col_count // row_count
    wanted = jnp.arange(local_cols) * stride + my_col // row_count
    chosen = factor.reshape(local_rows, BLK, PANEL)[wanted].reshape(local_cols * BLK, PANEL)
    across = broadcast(chosen, "row", my_col % row_count)
    trailing = assembled - jnp.dot(factor, across.T, precision=lax.Precision.HIGHEST)
    panel_col = lax.dynamic_slice_in_dim(
        factor, jnp.minimum(my_col, panel_blocks - 1) * BLK, BLK, 1
    )
    first_cols = jnp.where(my_col < panel_blocks, panel_col, trailing[:, :BLK])
    return jnp.concatenate([first_cols, trailing[:, BLK:]], axis=1)


def solution(mesh):
    placed = (P("row", "col"), P("row", "col"), P(), P())
    return jax.shard_map(
        local, mesh=mesh, in_specs=placed, out_specs=P("row", "col"), check_vma=False
    )
```

profile of v0, /device:TPU:13, one launch (start us, length us, event | category | flops | bytes accessed | tf_op | source)
XLA Modules:
  0.0 748.1 jit_solution(13739279627590797800)
XLA Ops:
  7.6 4.9 reshape.288
  12.6 8.4 %fusion.42 = f32[8,8,32768]{2,1,0:T(8,128)} fusion(f32[32,32768,1]{1,0,2:T(8,128)} %reshape.288, s32[32]{0:T(128)S(1)} %fusion.54, s32[8,8]{1,0:T(8,128)S(1)} %multiply_add_fusion.1), kind=kOutput, calls=%fused_computation.82 | convolution fusion | flops 805308416 | bytes 12583296 | tf_op jit(solution)/shard_map/dot_general | solution.py:43
  21.0 5.8 all-to-all-start
  27.5 6.2 copy.34
  34.5 85.8 %all-to-all-done = f32[8,8,32768]{2,1,0:T(8,128)} async-done(((f32[8,8,32768]{2,1,0:T(8,128)}), f32[8,8,32768]{2,1,0:T(8,128)}, u32[]{:S(2)}, u32[]{:S(2)}) %all-to-all-start) | async-done | bytes 8388640 | tf_op jit(solution)/shard_map/all_to_all | solution.py:46
  120.4 23.5 %fusion.14 = f32[8,8,128,2,128]{4,3,2,1,0:T(2,128)} fusion(f32[8,8,128,2,128]{4,1,3,2,0:T(8,128)} %bitcast.3, s32[8,2]{1,0:T(8,128)S(1)} %gather_fusion), kind=kOutput, calls=%fused_computation.24 | convolution fusion | flops 50331680 | bytes 16777280 | tf_op jit(solution)/shard_map/stq,smitj->smiqj/dot_general | solution.py:61
  143.9 11.5 %reshape.250 = f32[64,32768]{1,0:T(8,128)} reshape(f32[8,8,128,2,128]{4,3,2,1,0:T(2,128)} %fusion.14) | data formatting | bytes 16777216 | tf_op jit(solution)/shard_map/reshape | solution.py:62
  155.4 10.0 %fusion.59 = f32[44,32768]{1,0:T(8,128)} fusion(f32[44,64]{0,1:T(8,128)S(1)} %convolution_bitcast_fusion, f32[64,32768]{1,0:T(8,128)} %reshape.250), kind=kOutput, calls=%fused_computation.136 | convolution fusion | flops 1107296256 | bytes 14167040 | tf_op jit(solution)/shard_map/dot_general | solution.py:63
  165.4 7.0 reshape.251
  172.4 6.3 copy.35
  178.7 5.0 add.152
  183.7 5.3 slice_select_fusion
  189.8 166.4 %all-reduce.7.cloned.1.call-done = (f32[5632,128]{0,1:T(8,128)}, f32[5632,128]{0,1:T(8,128)}, f32[5632,128]{0,1:T(8,128)}, f32[5632,128]{0,1:T(8,128)}) async-done(((f32[5632,128]{0,1:T(8,128)}, f32[5632,128]{0,1:T(8,128)}, f32[5632,128]{0,1:T(8,128)}, f32[5632,128]{0,1:T(8,128)}), (f32[5632,128]{0,1:T(8,128)}, f32[5632,128]{0,1:T(8,128)}, f32[5632,128]{0,1:T(8,128)}, ...) | async-done | bytes 11534352 | tf_op jit(solution)/shard_map/psum | solution.py:12
  356.2 2.2 constant_dynamic-update-slice_fusion.3
  361.1 4.3 copy-done.1
  366.5 58.8 %all-gather.2.cloned.1.call-done = f32[1024,512]{0,1:T(8,128)} async-done(((f32[128,512]{0,1:T(8,128)}), f32[1024,512]{0,1:T(8,128)}) %all-gather.2.cloned.1.call-update) | async-done | bytes 2097168 | tf_op jit(solution)/shard_map/all_gather | solution.py:73
  426.9 1.4 fusion.22
  428.9 11.7 %cholesky.104 = f32[128,128]{1,0:T(8,128)S(1)} custom-call(f32[128,128]{1,0:T(8,128)S(1)} %cholesky.266), custom_call_target="Cholesky" | custom-call | tf_op jit(solution)/shard_map/jit(cholesky)/cholesky | solution.py:74
  440.7 9.8 %custom-call.31 = f32[1,128,128]{1,2,0:T(8,128)S(1)} custom-call(f32[1,128,128]{2,1,0:T(8,128)S(1)} %get-tuple-element.52), custom_call_target="InvertDiagBlocksLowerTriangular" | custom-call | tf_op jit(solution)/shard_map/jit(cholesky)/cholesky | solution.py:74
  451.2 11.7 %cholesky.217 = f32[128,128]{1,0:T(8,128)S(1)} custom-call(f32[128,128]{1,0:T(8,128)S(1)} %cholesky.270), custom_call_target="Cholesky" | custom-call | tf_op jit(solution)/shard_map/jit(cholesky)/cholesky | solution.py:74
  463.3 10.2 %custom-call.32 = f32[1,128,128]{1,2,0:T(8,128)S(1)} custom-call(f32[1,128,128]{2,1,0:T(8,128)S(1)} %get-tuple-element.50), custom_call_target="InvertDiagBlocksLowerTriangular" | custom-call | tf_op jit(solution)/shard_map/jit(cholesky)/cholesky | solution.py:74
  474.6 11.7 %cholesky.238 = f32[128,128]{1,0:T(8,128)S(1)} custom-call(f32[128,128]{1,0:T(8,128)S(1)} %cholesky.275), custom_call_target="Cholesky" | custom-call | tf_op jit(solution)/shard_map/jit(cholesky)/cholesky | solution.py:74
  486.4 9.8 %custom-call.33 = f32[1,128,128]{1,2,0:T(8,128)S(1)} custom-call(f32[1,128,128]{2,1,0:T(8,128)S(1)} %get-tuple-element.48), custom_call_target="InvertDiagBlocksLowerTriangular" | custom-call | tf_op jit(solution)/shard_map/jit(cholesky)/cholesky | solution.py:74
  497.0 11.9 %cholesky.255 = f32[128,128]{1,0:T(8,128)S(1)} custom-call(f32[128,128]{1,0:T(8,128)S(1)} %convolution_subtract_fusion.5), custom_call_target="Cholesky" | custom-call | tf_op jit(solution)/shard_map/jit(cholesky)/cholesky | solution.py:74
  513.6 1.7 fusion.23
  515.3 15.1 %while.1 = (s32[]{:T(128)}, f32[512,512]{0,1:T(8,128)}, s32[4,2]{0,1:T(2,128)S(1)}, f32[4,128,128]{2,1,0:T(8,128)}, s32[]{:T(128)}) while((s32[]{:T(128)}, f32[512,512]{0,1:T(8,128)}, s32[4,2]{0,1:T(2,128)S(1)}, f32[4,128,128]{2,1,0:T(8,128)}, s32[]{:T(128)}) %tuple.33), condition=%wide.while_cond, body=%wide.while_body.sunk | while | flops 2 | bytes 393829 | solution.py:16
  516.0 2.6 dynamic-slice.7
  520.0 2.3 dynamic-slice.7
  523.7 2.3 dynamic-slice.7
  527.4 2.3 dynamic-slice.7
  530.4 40.1 %custom-call.34 = f32[4,128,128]{1,2,0:T(8,128)S(1)} custom-call(f32[4,128,128]{2,1,0:T(8,128)} %get-tuple-element.12), custom_call_target="InvertDiagBlocksLowerTriangular" | custom-call | tf_op jit(solution)/shard_map/jit(_solve_triangular)/triangular_solve | solution.py:16
  570.6 4.6 fusion.19
  575.2 4.8 convolution_subtract_fusion.1
  580.0 2.7 fusion.35
  582.8 4.5 convolution_subtract_fusion.2
  587.4 3.0 fusion.33
  590.3 7.0 fusion.8
  597.3 2.7 fusion.32
  600.1 4.6 maximum_bitcast_fusion
  604.7 9.1 %slice.161 = f32[5504,512]{0,1:T(8,128)} slice(f32[5632,512]{0,1:T(8,128)} %maximum_bitcast_fusion), slice={[128:5632], [0:512]} | slice | bytes 22544384 | tf_op jit(solution)/shard_map/slice | solution.py:80
  614.8 9.3 %pad_maximum_fusion = f32[5632,512]{0,1:T(8,128)} fusion(f32[128,512]{0,1:T(8,128)S(1)} %slice_select_fusion.4, f32[5504,512]{0,1:T(8,128)} %slice.161), kind=kLoop, calls=%fused_computation.5 | loop fusion | flops 2883584 | bytes 23068672 | tf_op jit(solution)/shard_map/concatenate | solution.py:80
  624.1 12.2 %copy.46 = f32[5632,512]{1,0:T(8,128)} copy(f32[5632,512]{0,1:T(8,128)} %pad_maximum_fusion) | data formatting | bytes 23068672 | tf_op jit(solution)/shard_map/concatenate | solution.py:80
  636.4 4.9 gather_fusion.1
  642.1 72.9 %all-reduce.5.cloned.1.call-done = f32[256,512]{1,0:T(8,128)} async-done(((f32[256,512]{1,0:T(8,128)}), f32[256,512]{1,0:T(8,128)}) %all-reduce.5.cloned.1.call-update) | async-done | bytes 524304 | tf_op jit(solution)/shard_map/psum | solution.py:12
  715.0 14.7 %convolution_subtract_fusion = f32[5632,256]{0,1:T(8,128)S(1)} fusion(f32[5632,256]{0,1:T(8,128)} %copy-done, f32[256,512]{1,0:T(8,128)} %all-reduce.5.cloned.1.call-done, f32[128,512]{0,1:T(8,128)S(1)} %slice_select_fusion.4, f32[5504,512]{0,1:T(8,128)} %slice.161), kind=kOutput, calls=%fused_computation.16 | convolution fusion | flops 8862695424 | bytes 23592960 | tf_op jit(solution)/shard_map/dot_general | solution.py:85
  729.7 2.3 fusion.18
  732.0 2.9 pad_maximum_fusion.1
  734.9 6.2 copy.47
  (95 shorter events, 21.9 us)
Async XLA Ops:
  21.0 6.4 copy-start.5
  21.0 99.4 %all-to-all-start = ((f32[8,8,32768]{2,1,0:T(8,128)}), f32[8,8,32768]{2,1,0:T(8,128)}, u32[]{:S(2)}, u32[]{:S(2)}) async-start(f32[8,8,32768]{2,1,0:T(8,128)} %fusion.42), calls=%async_computation | async-start | bytes 16777216 | tf_op jit(solution)/shard_map/all_to_all | solution.py:46
  26.8 329.4 %all-reduce.7.cloned.1.call-start = ((), (), s32[]{:S(2)}) async-start(), calls=%async_computation.3 | async-start | bytes 23068672 | tf_op jit(solution)/shard_map/psum | solution.py:12
  183.7 6.0 copy-start
  189.7 235.5 %all-gather.2.cloned.1.call-start = ((), (), s32[]{:S(2)}) async-start(), calls=%async_computation.1 | async-start | bytes 2359296 | tf_op jit(solution)/shard_map/all_gather | solution.py:73
  356.2 2.7 copy-start.4
  356.2 3.6 copy-start.3
  358.9 2.0 copy-start.2
  361.1 4.4 copy-start.1
  366.2 348.8 %all-reduce.5.cloned.1.call-start = ((), (), s32[]{:S(2)}) async-start(), calls=%async_computation.2 | async-start | bytes 1048576 | tf_op jit(solution)/shard_map/psum | solution.py:12
  515.3 67.5 %slice-start = ((s8[11534336]{0:T(1024)(128)(4,1)}), s8[3145728]{0:T(1024)(128)(4,1)S(1)}, s32[]{:S(2)}) async-start(s8[11534336]{0:T(1024)(128)(4,1)} %bitcast.80), calls=%async_computation.4 | async-start | bytes 6291456
  570.5 12.2 %slice-start.1 = ((s8[11534336]{0:T(1024)(128)(4,1)}), s8[4194304]{0:T(1024)(128)(4,1)S(1)}, s32[]{:S(2)}) async-start(s8[11534336]{0:T(1024)(128)(4,1)} %bitcast.80), calls=%async_computation.5 | async-start | bytes 8388608
  575.2 7.6 %slice-start.2 = ((s8[11534336]{0:T(1024)(128)(4,1)}), s8[4194304]{0:T(1024)(128)(4,1)S(1)}, s32[]{:S(2)}) async-start(s8[11534336]{0:T(1024)(128)(4,1)} %bitcast.80), calls=%async_computation.6 | async-start | bytes 8388608
Sparse Core Ops, SparseCore 0:
  189.8 166.2 all-reduce.6
  366.3 58.8 all-gather.1
  642.2 72.7 all-reduce.4
where the time goes:
time: 758 us; the launch traced here: 748 us
  waiting for transfers between devices  384 us (51%)
  other arithmetic  154 us (20%)
  local copies, waits for them, and re-layouts  98.2 us (13%)
  matrix products  88.6 us (12%)
  between operations  16.6 us (2%)
    psum x2, waiting for transfers between devices, broadcast(): return lax.psum(jnp.where(mine, x, jnp.zeros_like(x)), axis)  239 us
    all_to_all x1, waiting for transfers between devices, local(): lax.all_to_all(outgoing, 'row', split_axis=0, concat_axis=0, tiled=True)  85.8 us
    another operation x14, other arithmetic, local(): lower_factor = jnp.linalg.cholesky((leading + leading.T) * 0.5)  79 us
    all_gather x1, waiting for transfers between devices, local(): lax.all_gather(panel_block[:BLK], 'row', axis=0, tiled=True)[:PANEL]  58.8 us
    another operation x3, other arithmetic, factor_rows(): jax.scipy.linalg.solve_triangular(lower_factor, panel_rows.T, lower=True)  41.8 us
    another operation x7, matrix products, factor_rows(): jax.scipy.linalg.solve_triangular(lower_factor, panel_rows.T, lower=True)  29.4 us
    dot_general x1, matrix products, local(): jnp.einsum('stq,smitj->smiqj', column_pick, received, precision=lax.Preci...  23.5 us
    unnamed x22, local copies, waits for them, and re-layouts  16 us
  transfers between devices with their start and end apart: 4, of which 4 were waited for; matrix products, arithmetic and copies ran while one was open for 1% of the time, Pallas kernels for 0%

commit v1 on v0

v1 whole, which is shorter than its diff:
```python
import jax
import jax.numpy as jnp
from jax import lax
from jax.experimental import pallas as pl
from jax.experimental.pallas import tpu as pltpu
from jax.sharding import PartitionSpec as P

BLK = 128
PANEL = 512
NR = 8
NC = 16
MOST = 8
SLOTS = NR * MOST
KR = 44
CHUNK = 4 * BLK
NCH = KR * BLK // CHUNK
HI = lax.Precision.HIGHEST
MESH = pl.DeviceIdType.MESH
F32 = jnp.float32
BF16 = jnp.bfloat16


def nt(a, b, precision=None):
    return lax.dot_general(
        a, b, (((1,), (1,)), ((), ())), precision=precision, preferred_element_type=F32
    )


def nn(a, b, precision=None):
    return lax.dot_general(
        a, b, (((1,), (0,)), ((), ())), precision=precision, preferred_element_type=F32
    )


def split(x):
    high = x.astype(BF16)
    return high, (x - high.astype(F32)).astype(BF16)


def inverse_of_factor(a):
    rows = lax.broadcasted_iota(jnp.int32, (BLK, 1), 0)
    eye = rows == lax.broadcasted_iota(jnp.int32, (BLK, BLK), 1)
    e = eye.astype(F32)
    done_a, done_e = [], []
    for first in range(0, BLK, 32):
        below = rows[first:]
        for j in range(first, first + 32):
            i = j - first
            pivot = 1.0 / a[i : i + 1, j : j + 1]
            col = jnp.where(below > j, a[:, j : j + 1], 0.0)
            row_a = a[i : i + 1, :] * pivot
            row_e = e[i : i + 1, :] * pivot
            a = a - col * row_a
            e = e - col * row_e
        done_a.append(a[:32])
        done_e.append(e[:32])
        a, e = a[32:], e[32:]
    a = jnp.concatenate(done_a, axis=0)
    e = jnp.concatenate(done_e, axis=0)
    d = jnp.sum(jnp.where(eye, a, 0.0), axis=1, keepdims=True)
    s = lax.rsqrt(d)
    s = s * (1.5 - 0.5 * d * s * s)
    return e * s


def kernel(
    tbl, front, children, out,
    stage0, stage1, in0, in1, panel, sbuf, psbuf, smat, xmat, wth, wtl,
    ex_send, ex_recv, own_sem, bc_send, bc_recv, s_send, s_recv, p_send, p_recv,
):
    r = lax.axis_index("row")
    c = lax.axis_index("col")
    x_hi = c // 8
    y = (c // 2) % 4
    core = c % 2
    is_panel = c < 4
    stages = (stage0, stage1)
    ins = (in0, in1)

    barrier = pltpu.get_barrier_semaphore()

    @pl.loop(1, NR)
    def _(i):
        pl.semaphore_signal(barrier, inc=1, device_id={"row": (r + i) % NR}, device_id_type=MESH)

    @pl.loop(1, NC)
    def _(i):
        pl.semaphore_signal(barrier, inc=1, device_id={"col": (c + i) % NC}, device_id_type=MESH)

    swap = tbl[SLOTS + 2 * KR] == 1

    def ex_copy(q, i):
        to = (r + i) % NR
        return pltpu.make_async_remote_copy(
            src_ref=stages[q].at[pl.ds(to * MOST, MOST)],
            dst_ref=ins[q].at[pl.ds(r * MOST, MOST)],
            send_sem=ex_send.at[q * NR + i],
            recv_sem=ex_recv.at[q * NR + i],
            device_id={"row": to},
            device_id_type=MESH,
        )

    def own_copy(q):
        return pltpu.make_async_copy(
            stages[q].at[pl.ds(r * MOST, MOST)], ins[q].at[pl.ds(r * MOST, MOST)], own_sem.at[q]
        )

    def fill(q, to):
        @pl.loop(0, MOST)
        def _(j):
            slot = to * MOST + j
            block = children[tbl[slot]]
            left, right = block[:, :BLK], block[:, BLK:]
            if q == 0:
                stages[q][slot] = jnp.where(swap, right, left)
            else:
                stages[q][slot] = jnp.where(swap, left, right)

    def assemble(q):
        cols = slice(q * BLK, (q + 1) * BLK)

        @pl.loop(0, KR)
        def _(k):
            at = pl.ds(pl.multiple_of(k * BLK, BLK), BLK)
            total = (
                front[at, cols] + ins[q][tbl[SLOTS + k]] + ins[q][tbl[SLOTS + KR + k]]
            )
            out[at, cols] = total
            if q == 0:

                @pl.when(is_panel)
                def _():
                    panel[c, at, :] = total

    fill(0, (r + 1) % NR)
    pl.semaphore_wait(barrier, NR - 1 + NC - 1)
    ex_copy(0, 1).start()

    @pl.loop(2, NR)
    def _(i):
        fill(0, (r + i) % NR)
        ex_copy(0, i).start()

    fill(0, r)
    own_copy(0).start()
    for q in range(2):
        ins[q][SLOTS] = jnp.zeros((BLK, BLK), F32)

    @pl.loop(0, NR)
    def _(i):
        fill(1, i)

    xmat[...] = jnp.zeros_like(xmat)
    own_copy(0).wait()

    @pl.loop(1, NR)
    def _(i):
        ex_copy(0, i).wait_recv()

    assemble(0)

    def bc_copy(s, i, d, to):
        at = pl.ds(pl.multiple_of(i * CHUNK, CHUNK), CHUNK)
        return pltpu.make_async_remote_copy(
            src_ref=panel.at[s, at],
            dst_ref=panel.at[s, at],
            send_sem=bc_send.at[(s * 4 + d) * NCH + i],
            recv_sem=bc_recv.at[s * NCH + i],
            device_id={"col": to},
            device_id_type=MESH,
        )

    def targets(g, i):
        yp = y if g == 0 else (5 - y) % 4
        even = i % 2 == 0
        odd = i % 2 == 1
        up, down = (yp + 1) % 4, (yp + 3) % 4
        y_up = up if g == 0 else (5 - up) % 4
        y_down = down if g == 0 else (5 - down) % 4
        here, there = x_hi == 0, x_hi == 1
        return (
            (
                (here & (yp == 0)) | (there & ((even & (yp == 0)) | (odd & (yp == 3)))),
                x_hi * 8 + y_up * 2 + core,
            ),
            (
                (yp == 3) | ((yp == 0) & (here | even)) | (there & odd & (yp == 2)),
                x_hi * 8 + y_down * 2 + core,
            ),
            (
                here & ((even & (yp == 0)) | (odd & (yp == 3))),
                8 + y * 2 + core,
            ),
            (core >= 0, x_hi * 8 + y * 2 + 1 - core),
        )

    def forward(i):
        for g in range(2):
            s = 2 * g + core

            @pl.when(c != s)
            def _():
                bc_copy(s, i, 0, c).wait_recv()

            for d, (when, to) in enumerate(targets(g, i)):

                @pl.when(when)
                def _():
                    bc_copy(s, i, d, to).start()

    def from_sibling(i):
        for g in range(2):
            s = 2 * g + 1 - core
            bc_copy(s, i, 0, c).wait_recv()

    forward(0)
    from_sibling(0)

    def s_copy(i):
        return pltpu.make_async_remote_copy(
            src_ref=panel.at[:, pl.ds(0, BLK)],
            dst_ref=sbuf.at[r],
            send_sem=s_send.at[i],
            recv_sem=s_recv.at[r],
            device_id={"row": (r + i) % NR},
            device_id_type=MESH,
        )

    def s_wait(source):
        pltpu.make_async_remote_copy(
            src_ref=panel.at[:, pl.ds(0, BLK)],
            dst_ref=sbuf.at[source],
            send_sem=s_send.at[0],
            recv_sem=s_recv.at[source],
            device_id={"row": r},
            device_id_type=MESH,
        ).wait_recv()

    def p_copy(i, k):
        at = pl.ds(pl.multiple_of((x_hi + 2 * k) * BLK, BLK), BLK)
        return pltpu.make_async_remote_copy(
            src_ref=panel.at[:, at],
            dst_ref=psbuf.at[k],
            send_sem=p_send.at[k * NR + i],
            recv_sem=p_recv.at[k],
            device_id={"row": (r + i) % NR},
            device_id_type=MESH,
        )

    is_lead = r < 4
    is_root = r == c % NR

    @pl.when(is_lead)
    def _():
        @pl.loop(1, NR)
        def _(i):
            s_copy(i).start()

        sbuf[r] = panel[:, pl.ds(0, BLK), :]

    @pl.when(is_root)
    def _():
        @pl.loop(1, NR)
        def _(i):
            for k in range(2):
                p_copy(i, k).start()

        for k in range(2):
            at = pl.ds(pl.multiple_of((x_hi + 2 * k) * BLK, BLK), BLK)
            psbuf[k] = panel[:, at, :]

    forward(1)
    forward(2)

    @pl.loop(0, 4)
    def _(source):
        @pl.when(source != r)
        def _():
            s_wait(source)

    @pl.loop(1, NR)
    def _(i):
        ex_copy(1, i).start()

    own_copy(1).start()

    for i in range(4):
        for j in range(4):
            smat[i * BLK : (i + 1) * BLK, j * BLK : (j + 1) * BLK] = 0.5 * (
                sbuf[i, j] + sbuf[j, i].T
            )

    @pl.loop(0, 4)
    def _(b):
        at = pl.ds(pl.multiple_of(b * BLK, BLK), BLK)
        x = xmat[...]
        lb = nt(smat[at, :], x, HI)
        block = smat[at, at] - nt(lb, lb, HI)
        v = inverse_of_factor(block)
        xmat[at, :] = -nn(v, nn(lb, x, HI), HI)
        xmat[at, at] = v
        forward(2 * b + 3)
        forward(2 * b + 4)

    @pl.when(jnp.logical_not(is_root))
    def _():
        for k in range(2):
            p_copy(0, k).wait_recv()

    for k in range(2):
        ps = jnp.concatenate([psbuf[k, s] for s in range(4)], axis=1)
        wt = nn(nt(ps, xmat[...], HI), xmat[...], HI)
        if k == 0:
            at = pl.ds(pl.multiple_of((c % 4) * BLK, BLK), BLK)
            wt = jnp.where(is_panel, -xmat[at, :], wt)
        high, low = split(wt)
        wth[k * BLK : (k + 1) * BLK, :] = high
        wtl[k * BLK : (k + 1) * BLK, :] = low

    own_copy(1).wait()

    @pl.loop(1, NR)
    def _(i):
        ex_copy(1, i).wait_recv()

    assemble(1)

    keep = jnp.where(
        is_panel & (lax.broadcasted_iota(jnp.int32, (1, 2 * BLK), 1) < BLK), 0.0, 1.0
    ).astype(F32)

    @pl.loop(1, NCH)
    def _(i):
        from_sibling(i)

    @pl.when(is_lead)
    def _():
        at = pl.ds(pl.multiple_of((r % 4) * BLK, BLK), BLK)
        for s in range(4):
            sbuf[0, s] = smat[at, s * BLK : (s + 1) * BLK]

    @pl.when(jnp.logical_not(is_lead))
    def _():
        for s in range(4):
            sbuf[0, s] = panel[s, 0:BLK, :]

    def update(parts, at):
        rows = jnp.concatenate(parts, axis=1)
        high, low = split(rows)
        total = nt(high, wth[...]) + (nt(high, wtl[...]) + nt(low, wth[...]))
        out[at, :] = out[at, :] * keep - total

    update([sbuf[0, s] for s in range(4)], pl.ds(0, BLK))
    update([panel[s, BLK : 2 * BLK, :] for s in range(4)], pl.ds(BLK, BLK))

    @pl.loop(1, KR // 2)
    def _(k):
        at = pl.ds(pl.multiple_of(k * 2 * BLK, 2 * BLK), 2 * BLK)
        update([panel[s, at, :] for s in range(4)], at)

    @pl.loop(1, NR)
    def _(i):
        for q in range(2):
            ex_copy(q, i).wait_send()

    @pl.when(is_lead)
    def _():
        @pl.loop(1, NR)
        def _(i):
            s_copy(i).wait_send()

    @pl.when(is_root)
    def _():
        @pl.loop(1, NR)
        def _(i):
            for k in range(2):
                p_copy(i, k).wait_send()

    @pl.loop(0, NCH)
    def _(i):
        for g in range(2):
            for d, (when, to) in enumerate(targets(g, i)):

                @pl.when(when)
                def _():
                    bc_copy(2 * g + core, i, d, to).wait_send()


def tables(row_map, col_map):
    my_row = lax.axis_index("row")
    my_col = lax.axis_index("col")
    layout = row_map.reshape(NR, -1)
    count = layout.shape[1]
    owner = layout % NR
    counter = jnp.arange(count)
    earlier = (owner[:, :, None] == owner[:, None, :]) & (
        counter[None, None, :] < counter[None, :, None]
    )
    rank = jnp.sum(earlier.astype(jnp.int32), axis=2)
    slot_out = owner * MOST + rank
    mine = lax.dynamic_index_in_dim(slot_out, my_row, 0, keepdims=False)
    send = jnp.sum(
        jnp.where(mine[None, :] == jnp.arange(SLOTS)[:, None], counter[None, :], 0), axis=1
    )
    slot_in = (jnp.arange(NR)[:, None] * MOST + rank).reshape(2, -1)
    wanted = jnp.arange(KR) * NR + my_row
    hit = layout.reshape(2, 1, -1) == wanted[None, :, None]
    receive = SLOTS + jnp.sum(jnp.where(hit, slot_in[:, None, :] - SLOTS, 0), axis=2)
    child = my_row // (NR // 2)
    first = lax.dynamic_index_in_dim(
        col_map.reshape(2, NC, 2)[:, :, 0].reshape(-1), child * NC + my_col, 0
    )
    return jnp.concatenate([send, receive.reshape(-1), first // NC]).astype(jnp.int32)


def local(front, children, row_map, col_map):
    table = tables(row_map, col_map)
    vmem = pl.BlockSpec(memory_space=pltpu.VMEM)
    rows = front.shape[0]
    blocks = children.reshape(-1, BLK, 2 * BLK)
    tile = (BLK, BLK)
    return pl.pallas_call(
        kernel,
        out_shape=jax.ShapeDtypeStruct(front.shape, F32),
        in_specs=[pl.BlockSpec(memory_space=pltpu.SMEM), vmem, vmem],
        out_specs=vmem,
        scratch_shapes=[
            pltpu.VMEM((SLOTS,) + tile, F32),
            pltpu.VMEM((SLOTS,) + tile, F32),
            pltpu.VMEM((SLOTS + 1,) + tile, F32),
            pltpu.VMEM((SLOTS + 1,) + tile, F32),
            pltpu.VMEM((4, rows, BLK), F32),
            pltpu.VMEM((4, 4) + tile, F32),
            pltpu.VMEM((2, 4) + tile, F32),
            pltpu.VMEM((PANEL, PANEL), F32),
            pltpu.VMEM((PANEL, PANEL), F32),
            pltpu.VMEM((2 * BLK, PANEL), BF16),
            pltpu.VMEM((2 * BLK, PANEL), BF16),
            pltpu.SemaphoreType.DMA((2 * NR,)),
            pltpu.SemaphoreType.DMA((2 * NR,)),
            pltpu.SemaphoreType.DMA((2,)),
            pltpu.SemaphoreType.DMA((16 * NCH,)),
            pltpu.SemaphoreType.DMA((4 * NCH,)),
            pltpu.SemaphoreType.DMA((NR,)),
            pltpu.SemaphoreType.DMA((4,)),
            pltpu.SemaphoreType.DMA((2 * NR,)),
            pltpu.SemaphoreType.DMA((2,)),
        ],
        compiler_params=pltpu.CompilerParams(
            collective_id=0, has_side_effects=True, vmem_limit_bytes=60 * 2**20
        ),
    )(table, front, blocks)


def solution(mesh):
    placed = (P("row", "col"), P("row", "col"), P(), P())
    return jax.shard_map(
        local, mesh=mesh, in_specs=placed, out_specs=P("row", "col"), check_vma=False
    )
```

time: 758 us -> 394 us (0.52)
  the two profiles are of different devices: /device:TPU:13 before, /device:TPU:28 now
where the time goes in v1:
time: 394 us
  Pallas kernels  381 us (97%)
  local copies, waits for them, and re-layouts  8.25 us (2%)
    pallas_call x1, Pallas kernels, local(): pl.pallas_call(kernel, out_shape=jax.ShapeDtypeStruct(front.shape, F32),...  381 us

profile of v1, /device:TPU:28, one launch (start us, length us, event | category | flops | bytes accessed | tf_op | source)
XLA Modules:
  0.0 394.3 jit_solution(14191371405813185529)
XLA Ops:
  0.0 0.1 add.77
  0.1 0.1 add.78
  0.2 0.8 reshape.101
  0.9 0.3 convert_reduce_fusion
  1.3 0.1 reduce_sum.31
  1.4 0.1 select_reduce_fusion
  1.5 0.7 reshape.102
  2.2 0.1 slice_reduce_fusion
  2.3 0.1 reshape_squeeze.3
  2.4 0.6 dynamic_slice.9
  5.6 1.6 fusion
  7.2 0.1 copy.7
  7.3 0.1 add.82
  7.4 0.6 pad_add_fusion.tbl
  8.0 380.7 %shard_map.46 = f32[5632,256]{1,0:T(8,128)} custom-call(s32[153]{0:T(256)} %pad_add_fusion.tbl, f32[5632,256]{1,0:T(8,128)} %front.1, f32[32,128,256]{2,1,0:T(8,128)} %bitcast.4), custom_call_target="tpu_custom_call" | custom-call | tf_op jit(solution)/shard_map/pallas_call | solution.py:422
  388.7 5.5 %copy.9 = f32[5632,256]{1,0:T(8,128)} copy(f32[5632,256]{1,0:T(8,128)} %shard_map.46) | data formatting | bytes 11534336
  (8 shorter events, 0.1 us)

commit v2 on v1

v2 whole, which is shorter than its diff:
```python
import jax
import jax.numpy as jnp
from jax import lax
from jax.experimental import pallas as pl
from jax.experimental.pallas import tpu as pltpu
from jax.sharding import PartitionSpec as P

BLK = 128
PANEL = 512
NR = 8
NC = 16
MOST = 8
SLOTS = NR * MOST
KR = 44
SUB = 4
PART = BLK // SUB
SPAN = KR * PART
NCH = (PANEL + KR * BLK) // BLK
LEAD = PANEL // BLK
TURN = SPAN // BLK
UNIT = 11
WINDOW = 6
LAG = 4
STEPS = NCH + 4 * LAG
AHEAD = LEAD + 2 * TURN
HI = lax.Precision.HIGHEST
MESH = pl.DeviceIdType.MESH
F32 = jnp.float32
BF16 = jnp.bfloat16


def nt(a, b, precision=None):
    return lax.dot_general(
        a, b, (((1,), (1,)), ((), ())), precision=precision, preferred_element_type=F32
    )


def nn(a, b, precision=None):
    return lax.dot_general(
        a, b, (((1,), (0,)), ((), ())), precision=precision, preferred_element_type=F32
    )


def split(x):
    high = x.astype(BF16)
    return high, (x - high.astype(F32)).astype(BF16)


def inverse_of_factor(a, between):
    rows = lax.broadcasted_iota(jnp.int32, (BLK, 1), 0)
    eye = rows == lax.broadcasted_iota(jnp.int32, (BLK, BLK), 1)
    e = eye.astype(F32)
    done_a, done_e = [], []
    for first in range(0, BLK, 32):
        below = rows[first:]
        for j in range(first, first + 32):
            i = j - first
            pivot = 1.0 / a[i : i + 1, j : j + 1]
            col = jnp.where(below > j, a[:, j : j + 1], 0.0)
            row_a = a[i : i + 1, :] * pivot
            row_e = e[i : i + 1, :] * pivot
            a = a - col * row_a
            e = e - col * row_e
        done_a.append(a[:32])
        done_e.append(e[:32])
        a, e = a[32:], e[32:]
        between(first // 32)
    a = jnp.concatenate(done_a, axis=0)
    e = jnp.concatenate(done_e, axis=0)
    d = jnp.sum(jnp.where(eye, a, 0.0), axis=1, keepdims=True)
    s = lax.rsqrt(d)
    s = s * (1.5 - 0.5 * d * s * s)
    return e * s


def kernel(
    tbl, front, children_hbm, out,
    children, acc, stage0, stage1, in00, in01, in02, in03, in10, in11, in12, in13, stage_s, in_s, panel, psbuf, smat, xmat, block, lbx, wth, wtl,
    load_sem, ex_send, ex_recv, own_sem, bc_send, bc_recv, se_send, se_recv, s_send, s_recv, p_send, p_recv, out_sem,
):
    r = lax.axis_index("row")
    c = lax.axis_index("col")
    x_hi = c // 8
    y = (c // 2) % 4
    core = c % 2
    is_panel = c < 4
    is_lead = r < 4
    is_root = r == c % NR
    ins = (in00, in01, in02, in03, in10, in11, in12, in13)

    load_children = pltpu.make_async_copy(children_hbm, children, load_sem.at[0])
    load_front = pltpu.make_async_copy(front, acc, load_sem.at[1])
    load_children.start()
    load_front.start()

    barrier = pltpu.get_barrier_semaphore()

    @pl.loop(1, NR)
    def _(i):
        pl.semaphore_signal(barrier, inc=1, device_id={"row": (r + i) % NR}, device_id_type=MESH)

    @pl.loop(1, NC)
    def _(i):
        pl.semaphore_signal(barrier, inc=1, device_id={"col": (c + i) % NC}, device_id_type=MESH)

    swap = tbl[SLOTS + 2 * KR] == 1

    def ex_parts(t, slots):
        at = pl.ds(t % SUB * PART, PART)
        return (stage0 if t < SUB else stage1).at[slots, at]

    def ex_copy(t, i):
        to = (r + i) % NR
        return pltpu.make_async_remote_copy(
            src_ref=ex_parts(t, pl.ds(to * MOST, MOST)),
            dst_ref=ins[t].at[pl.ds(r * MOST, MOST)],
            send_sem=ex_send.at[t * NR + i],
            recv_sem=ex_recv.at[t * NR + i],
            device_id={"row": to},
            device_id_type=MESH,
        )

    def own_copy(t):
        mine = pl.ds(r * MOST, MOST)
        return pltpu.make_async_copy(ex_parts(t, mine), ins[t].at[mine], own_sem.at[t])

    def send_part(t):
        own_copy(t).start()

        @pl.loop(1, NR)
        def _(i):
            ex_copy(t, i).start()

    def sent_part(t):
        @pl.loop(1, NR)
        def _(i):
            ex_copy(t, i).wait_send()

    def got_part(t):
        own_copy(t).wait()

        @pl.loop(1, NR)
        def _(i):
            ex_copy(t, i).wait_recv()

    def se_copy(d):
        return pltpu.make_async_remote_copy(
            src_ref=stage_s.at[d],
            dst_ref=in_s.at[r],
            send_sem=se_send.at[d],
            recv_sem=se_recv.at[r],
            device_id={"row": d},
            device_id_type=MESH,
        )

    def se_wait(source):
        pltpu.make_async_remote_copy(
            src_ref=stage_s.at[0],
            dst_ref=in_s.at[source],
            send_sem=se_send.at[0],
            recv_sem=se_recv.at[source],
            device_id={"row": r},
            device_id_type=MESH,
        ).wait_recv()

    load_children.wait()

    @pl.loop(0, LEAD)
    def _(d):
        found = tbl[SLOTS + 2 * KR + 1 + d]
        block = children[jnp.maximum(found - 1, 0)]
        half = jnp.where(swap, block[:, BLK:], block[:, :BLK])
        stage_s[d] = jnp.where(found > 0, half, 0.0)

    pl.semaphore_wait(barrier, NR - 1 + NC - 1)

    @pl.when(is_panel)
    def _():
        @pl.loop(0, LEAD)
        def _(d):
            @pl.when(d != r)
            def _():
                se_copy(d).start()

    @pl.loop(0, SLOTS)
    def _(slot):
        block = children[tbl[slot]]
        stage0[slot] = jnp.where(swap, block[:, BLK:], block[:, :BLK])

    send_part(0)
    for t in range(2 * SUB):
        ins[t][SLOTS] = jnp.zeros((PART, BLK), F32)

    @pl.loop(0, SLOTS)
    def _(slot):
        block = children[tbl[slot]]
        stage1[slot] = jnp.where(swap, block[:, :BLK], block[:, BLK:])

    xmat[...] = jnp.zeros_like(xmat)
    load_front.wait()

    def s_copy(i):
        at = pl.ds(pl.multiple_of(r * BLK, BLK), BLK)
        return pltpu.make_async_remote_copy(
            src_ref=panel.at[c, at],
            dst_ref=panel.at[c, at],
            send_sem=s_send.at[i],
            recv_sem=s_recv.at[r],
            device_id={"row": (r + i) % NR},
            device_id_type=MESH,
        )

    def s_wait(source):
        at = pl.ds(pl.multiple_of(source * BLK, BLK), BLK)
        pltpu.make_async_remote_copy(
            src_ref=panel.at[c, at],
            dst_ref=panel.at[c, at],
            send_sem=s_send.at[0],
            recv_sem=s_recv.at[source],
            device_id={"row": r},
            device_id_type=MESH,
        ).wait_recv()

    @pl.when(is_panel & is_lead)
    def _():
        in_s[r] = stage_s[r]

        @pl.loop(0, NR)
        def _(source):
            @pl.when(source != r)
            def _():
                se_wait(source)

        total = acc[0, :, :BLK]
        for source in range(NR):
            total = total + in_s[source]
        panel[c, pl.ds(pl.multiple_of(r * BLK, BLK), BLK), :] = total

        @pl.loop(1, NR)
        def _(i):
            s_copy(i).start()

    @pl.when(is_panel)
    def _():
        @pl.loop(0, LEAD)
        def _(source):
            @pl.when(source != r)
            def _():
                s_wait(source)

    def bc_copy(s, i, d, to):
        at = pl.ds(pl.multiple_of(i * BLK, BLK), BLK)
        return pltpu.make_async_remote_copy(
            src_ref=panel.at[s, at],
            dst_ref=panel.at[s, at],
            send_sem=bc_send.at[(s * 4 + d) * NCH + i],
            recv_sem=bc_recv.at[s * NCH + i],
            device_id={"col": to},
            device_id_type=MESH,
        )

    def targets(g, i):
        yp = y if g == 0 else (5 - y) % 4
        even = i % 2 == 0
        odd = i % 2 == 1
        up, down = (yp + 1) % 4, (yp + 3) % 4
        y_up = up if g == 0 else (5 - up) % 4
        y_down = down if g == 0 else (5 - down) % 4
        here, there = x_hi == 0, x_hi == 1
        return (
            (
                (here & (yp == 0)) | (there & ((even & (yp == 0)) | (odd & (yp == 3)))),
                x_hi * 8 + y_up * 2 + core,
            ),
            (
                (yp == 3) | ((yp == 0) & (here | even)) | (there & odd & (yp == 2)),
                x_hi * 8 + y_down * 2 + core,
            ),
            (
                here & ((even & (yp == 0)) | (odd & (yp == 3))),
                8 + y * 2 + core,
            ),
            (core >= 0, x_hi * 8 + y * 2 + 1 - core),
        )

    def sent(g, i):
        for d, (when, to) in enumerate(targets(g, i)):

            @pl.when(when)
            def _():
                bc_copy(2 * g + core, i, d, to).wait_send()

    def forward(step):
        odd = step % 2
        for g in range(2):
            s = 2 * g + core
            yp = y if g == 0 else (5 - y) % 4
            near = jnp.where(yp == 0, 0, jnp.where(yp == 2, 2, 1))
            far_odd = jnp.where(yp == 3, 2, jnp.where(yp == 1, 4, 3))
            far = jnp.where(odd == 1, far_odd, near + 1)
            i = step - LAG * jnp.where(x_hi == 0, near, far)

            @pl.when((i >= 0) & (i < NCH))
            def _():
                @pl.when(c != s)
                def _():
                    bc_copy(s, i, 0, c).wait_recv()

                @pl.when((c == s) & (i >= WINDOW))
                def _():
                    sent(g, i - WINDOW)

                for d, (when, to) in enumerate(targets(g, i)):

                    @pl.when(when)
                    def _():
                        bc_copy(s, i, d, to).start()

    def from_sibling(i):
        for g in range(2):
            s = 2 * g + 1 - core
            bc_copy(s, i, 0, c).wait_recv()

    def forward_all(first, last):
        @pl.loop(first, last)
        def _(step):
            forward(step)

    def assemble(t, store):
        q, part = t // SUB, pl.ds(t % SUB * PART, PART)

        @pl.loop(0, KR)
        def _(k):
            total = (
                acc[k, part, q * BLK : (q + 1) * BLK]
                + ins[t][tbl[SLOTS + k]]
                + ins[t][tbl[SLOTS + KR + k]]
            )
            store(k, total)

    def assemble_here(t):
        q, part = t // SUB, pl.ds(t % SUB * PART, PART)

        def store(k, total):
            acc[k, part, q * BLK : (q + 1) * BLK] = total

        assemble(t, store)

    def phase(t):
        if t == 0:
            sent_part(0)
        if t < SUB - 1:
            send_part(t + 1)
        got_part(t)

        def store(k, total):
            at = pl.ds(pl.multiple_of(PANEL + t * SPAN + k * PART, PART), PART)
            panel[c, at, :] = total

        @pl.when(is_panel)
        def _():
            assemble(t, store)

        @pl.when(jnp.logical_not(is_panel))
        def _():
            assemble_here(t)

    def second(t):
        if t < SUB - 1:
            sent_part(t + 1)
        send_part(SUB + t)

    def p_copy(i, k, t):
        at = pl.ds(pl.multiple_of(PANEL + t * SPAN + (x_hi + 2 * k) * PART, PART), PART)
        return pltpu.make_async_remote_copy(
            src_ref=panel.at[:, at],
            dst_ref=psbuf.at[k, :, pl.ds(t * PART, PART)],
            send_sem=p_send.at[(t * 2 + k) * NR + i],
            recv_sem=p_recv.at[t * 2 + k],
            device_id={"row": (r + i) % NR},
            device_id_type=MESH,
        )

    def send_rows(t):
        from_sibling(LEAD + t * TURN)

        @pl.when(is_root)
        def _():
            @pl.loop(1, NR)
            def _(i):
                for k in range(2):
                    p_copy(i, k, t).start()

            for k in range(2):
                at = pl.ds(pl.multiple_of(PANEL + t * SPAN + (x_hi + 2 * k) * PART, PART), PART)
                psbuf[k, :, t * PART : (t + 1) * PART, :] = panel[:, at, :]

    forward_all(0, LEAD)
    phase(0)
    forward_all(LEAD, LEAD + TURN // 2)
    second(0)
    forward_all(LEAD + TURN // 2, LEAD + TURN)
    phase(1)
    forward_all(LEAD + TURN, LEAD + TURN + TURN // 2)
    second(1)
    forward_all(LEAD + TURN + TURN // 2, AHEAD)
    for i in range(LEAD):
        from_sibling(i)

    send_rows(0)
    for i in range(4):
        for j in range(4):
            rows = slice(i * BLK, (i + 1) * BLK)
            cols = slice(j * BLK, (j + 1) * BLK)
            smat[rows, cols] = 0.5 * (panel[j, rows, :] + panel[i, cols, :].T)

    @pl.loop(0, 4)
    def _(b):
        for t in range(2, SUB):

            @pl.when(b == t - 2)
            def _():
                phase(t)

        at = pl.ds(pl.multiple_of(b * BLK, BLK), BLK)
        block[...] = smat[at, at]
        for k in range(1, 4):

            @pl.when(b == k)
            def _():
                x = xmat[: k * BLK, : k * BLK]
                lb = nt(smat[k * BLK : (k + 1) * BLK, : k * BLK], x, HI)
                block[...] -= nt(lb, lb, HI)
                lbx[:, : k * BLK] = nn(lb, x, HI)

        def between(n):
            first = AHEAD + 8 * b + 2 * n
            forward_all(first, first + 2)
            @pl.when((b == 0) & (n == 2))
            def _():
                second(2)

            @pl.when((b == 1) & (n == 1))
            def _():
                second(3)

            for t in range(1, SUB):
                due = LEAD + t * TURN + 4 * LAG - AHEAD - 1
                due = -(-due // 2)

                @pl.when(4 * b + n == due)
                def _():
                    send_rows(t)

        v = inverse_of_factor(block[...], between)
        for k in range(1, 4):

            @pl.when(b == k)
            def _():
                xmat[k * BLK : (k + 1) * BLK, : k * BLK] = -nn(v, lbx[:, : k * BLK], HI)

        xmat[at, at] = v

    last = AHEAD + 32
    forward_all(last, last + 2)

    @pl.when(jnp.logical_not(is_root))
    def _():
        for t in range(SUB):
            for k in range(2):
                p_copy(0, k, t).wait_recv()

    x_high, x_low = split(xmat[...])

    def three(product, a, high, low):
        a_high, a_low = split(a)
        return product(a_high, high) + (product(a_high, low) + product(a_low, high))

    for k in range(2):
        ps = jnp.concatenate([psbuf[k, s] for s in range(4)], axis=1)
        wt = three(nn, three(nt, ps, x_high, x_low), x_high, x_low)
        if k == 0:
            at = pl.ds(pl.multiple_of((c % 4) * BLK, BLK), BLK)
            wt = jnp.where(is_panel, -xmat[at, :], wt)
        high, low = split(wt)
        wth[k * BLK : (k + 1) * BLK, :] = high
        wtl[k * BLK : (k + 1) * BLK, :] = low

    forward_all(last + 2, last + 3)

    for t in range(SUB, 2 * SUB):
        got_part(t)
        assemble_here(t)

    forward_all(last + 3, last + 4)
    drop = is_panel & (lax.broadcasted_iota(jnp.int32, (1, 2 * BLK), 1) < BLK)

    def out_copy(t, u):
        return pltpu.make_async_copy(
            acc.at[pl.ds(u * UNIT, UNIT), pl.ds(t * PART, PART)],
            out.at[pl.ds(u * UNIT, UNIT), pl.ds(t * PART, PART)],
            out_sem.at[t * 4 + u],
        )

    def update(t):
        @pl.loop(1, TURN)
        def _(i):
            from_sibling(LEAD + t * TURN + i)

        @pl.loop(0, KR // UNIT)
        def _(u):
            first = pl.multiple_of(PANEL + t * SPAN + u * UNIT * PART, PART)
            rows = jnp.concatenate(
                [panel[s, pl.ds(first, UNIT * PART), :] for s in range(4)], axis=1
            )
            lead_at = pl.ds(pl.multiple_of((r % 4) * BLK + t * PART, PART), PART)
            head = jnp.where(is_lead & (u == 0), smat[lead_at, :], rows[:PART])
            rows = jnp.concatenate([head, rows[PART:]], axis=0)
            high, low = split(rows)
            total = nt(high, wth[...]) + (nt(high, wtl[...]) + nt(low, wth[...]))
            for b in range(UNIT):
                at = u * UNIT + b
                part = slice(t * PART, (t + 1) * PART)
                acc[at, part, :] = (
                    jnp.where(drop, 0.0, acc[at, part, :]) - total[b * PART : (b + 1) * PART]
                )
            out_copy(t, u).start()

    update(0)
    forward_all(last + 4, last + 5)
    update(1)
    forward_all(last + 5, STEPS)
    update(2)
    update(3)

    for t in range(SUB):

        @pl.loop(0, KR // UNIT)
        def _(u):
            out_copy(t, u).wait()

        sent_part(SUB + t)

    @pl.when(is_panel)
    def _():
        @pl.loop(0, LEAD)
        def _(d):
            @pl.when(d != r)
            def _():
                se_copy(d).wait_send()

    @pl.when(is_panel & is_lead)
    def _():
        @pl.loop(1, NR)
        def _(i):
            s_copy(i).wait_send()

    @pl.when(is_root)
    def _():
        @pl.loop(1, NR)
        def _(i):
            for t in range(SUB):
                for k in range(2):
                    p_copy(i, k, t).wait_send()

    for g in range(2):

        @pl.loop(0, NCH)
        def _(i):
            @pl.when((c != 2 * g + core) | (i >= NCH - WINDOW))
            def _():
                sent(g, i)


def tables(row_map, col_map):
    my_row = lax.axis_index("row")
    my_col = lax.axis_index("col")
    layout = row_map.reshape(NR, -1)
    count = layout.shape[1]
    owner = layout % NR
    counter = jnp.arange(count)
    earlier = (owner[:, :, None] == owner[:, None, :]) & (
        counter[None, None, :] < counter[None, :, None]
    )
    rank = jnp.sum(earlier.astype(jnp.int32), axis=2)
    slot_out = owner * MOST + rank
    mine = lax.dynamic_index_in_dim(slot_out, my_row, 0, keepdims=False)
    send = jnp.sum(
        jnp.where(mine[None, :] == jnp.arange(SLOTS)[:, None], counter[None, :], 0), axis=1
    )
    slot_in = (jnp.arange(NR)[:, None] * MOST + rank).reshape(2, -1)
    wanted = jnp.arange(KR) * NR + my_row
    hit = layout.reshape(2, 1, -1) == wanted[None, :, None]
    receive = SLOTS + jnp.sum(jnp.where(hit, slot_in[:, None, :] - SLOTS, 0), axis=2)
    child = my_row // (NR // 2)
    first = lax.dynamic_index_in_dim(
        col_map.reshape(2, NC, 2)[:, :, 0].reshape(-1), child * NC + my_col, 0
    )
    own = lax.dynamic_index_in_dim(layout, my_row, 0, keepdims=False)
    lead = jnp.sum(
        jnp.where(own[None, :] == jnp.arange(LEAD)[:, None], counter[None, :] + 1, 0), axis=1
    )
    return jnp.concatenate([send, receive.reshape(-1), first // NC, lead]).astype(jnp.int32)


def local(front, children, row_map, col_map):
    table = tables(row_map, col_map)
    hbm = pl.BlockSpec(memory_space=pl.ANY)
    blocks = children.reshape(-1, BLK, 2 * BLK)
    tile = (BLK, BLK)
    held = front.reshape(KR, BLK, 2 * BLK)
    vmem = lambda *shape: pltpu.VMEM(shape, F32)
    dma = lambda count: pltpu.SemaphoreType.DMA((count,))
    result = pl.pallas_call(
        kernel,
        out_shape=jax.ShapeDtypeStruct(held.shape, F32),
        in_specs=[pl.BlockSpec(memory_space=pltpu.SMEM), hbm, hbm],
        out_specs=hbm,
        scratch_shapes=[
            vmem(*blocks.shape),
            vmem(*held.shape),
            vmem(SLOTS, *tile),
            vmem(SLOTS, *tile),
            *[vmem(SLOTS + 1, PART, BLK) for _ in range(2 * SUB)],
            vmem(LEAD, *tile),
            vmem(NR, *tile),
            vmem(4, NCH * BLK, BLK),
            vmem(2, 4, *tile),
            vmem(PANEL, PANEL),
            vmem(PANEL, PANEL),
            vmem(*tile),
            vmem(BLK, PANEL),
            pltpu.VMEM((2 * BLK, PANEL), BF16),
            pltpu.VMEM((2 * BLK, PANEL), BF16),
            dma(2),
            dma(2 * SUB * NR),
            dma(2 * SUB * NR),
            dma(2 * SUB),
            dma(16 * NCH),
            dma(4 * NCH),
            dma(LEAD),
            dma(NR),
            dma(NR),
            dma(LEAD),
            dma(2 * SUB * NR),
            dma(2 * SUB),
            dma(16),
        ],
        compiler_params=pltpu.CompilerParams(
            collective_id=0, has_side_effects=True, vmem_limit_bytes=60 * 2**20
        ),
    )(table, held, blocks)
    return result.reshape(front.shape)


def solution(mesh):
    placed = (P("row", "col"), P("row", "col"), P(), P())
    return jax.shard_map(
        local, mesh=mesh, in_specs=placed, out_specs=P("row", "col"), check_vma=False
    )
```

time: 394 us -> 220 us (0.56)
  the two profiles are of different devices: /device:TPU:28 before, /device:TPU:13 now
where the time goes in v2:
time: 220 us; the launch traced here: 217 us
  Pallas kernels  203 us (92%)
  local copies, waits for them, and re-layouts  8.25 us (4%)
  other arithmetic  2.77 us (1%)
  between operations  2.67 us (1%)
    pallas_call x1, Pallas kernels, local(): pl.pallas_call(kernel, out_shape=jax.ShapeDtypeStruct(held.shape, F32), i...  203 us
    unnamed x2, local copies, waits for them, and re-layouts  5.62 us

profile of v2, /device:TPU:13, one launch (start us, length us, event | category | flops | bytes accessed | tf_op | source)
XLA Modules:
  0.0 216.8 jit_solution(4855750073869481441)
XLA Ops:
  0.0 0.1 add.89
  0.1 0.1 add.90
  0.2 0.8 reshape.112
  1.0 0.3 convert_reduce_fusion
  1.3 0.1 reduce_sum.40
  1.4 0.1 select_reduce_fusion.1
  1.5 0.1 select_reduce_fusion
  1.6 0.8 reshape.113
  2.3 0.1 slice_reduce_fusion
  2.5 0.1 reshape_squeeze.3
  2.5 0.6 dynamic_slice.12
  5.7 1.6 fusion
  7.3 0.1 copy.7
  7.4 0.1 add.94
  7.5 0.6 pad_add_fusion.tbl
  8.1 203.1 %shard_map.46 = f32[44,128,256]{2,1,0:T(8,128)} custom-call(s32[157]{0:T(256)} %pad_add_fusion.tbl, f32[44,128,256]{2,1,0:T(8,128)} %bitcast.9, f32[32,128,256]{2,1,0:T(8,128)} %bitcast.10), custom_call_target="tpu_custom_call" | custom-call | tf_op jit(solution)/shard_map/pallas_call | solution.py:614
  211.2 5.5 %copy.9 = f32[5632,256]{1,0:T(8,128)} copy(f32[5632,256]{1,0:T(8,128)} %bitcast.8) | data formatting | bytes 11534336
  (9 shorter events, 0.1 us)

commit v3 on v2

--- a/solution.py
+++ b/solution.py
@@ -21,6 +21,9 @@
 UNIT = 11
 WINDOW = 6
 LAG = 4
+SEND_5 = 3
+SEND_6 = 12
+SEND_7 = 14
 STEPS = NCH + 4 * LAG
 AHEAD = LEAD + 2 * TURN
 HI = lax.Precision.HIGHEST
@@ -196,6 +199,10 @@
         block = children[tbl[slot]]
         stage1[slot] = jnp.where(swap, block[:, :BLK], block[:, BLK:])
 
+    @pl.when(jnp.logical_not(is_panel))
+    def _():
+        send_part(1)
+
     xmat[...] = jnp.zeros_like(xmat)
     load_front.wait()
 
@@ -242,6 +249,8 @@
 
     @pl.when(is_panel)
     def _():
+        send_part(1)
+
         @pl.loop(0, LEAD)
         def _(source):
             @pl.when(source != r)
@@ -347,10 +356,8 @@
         assemble(t, store)
 
     def phase(t):
-        if t == 0:
-            sent_part(0)
-        if t < SUB - 1:
-            send_part(t + 1)
+        if t < 2:
+            send_part(t + 2)
         got_part(t)
 
         def store(k, total):
@@ -365,44 +372,69 @@
         def _():
             assemble_here(t)
 
-    def second(t):
-        if t < SUB - 1:
-            sent_part(t + 1)
-        send_part(SUB + t)
-
-    def p_copy(i, k, t):
-        at = pl.ds(pl.multiple_of(PANEL + t * SPAN + (x_hi + 2 * k) * PART, PART), PART)
+    other = r + 1 - 2 * (r % 2)
+    is_relay = other == c % NR
+
+    def p_rows(k, t):
+        return pl.ds(pl.multiple_of(PANEL + t * SPAN + (x_hi + 2 * k) * PART, PART), PART)
+
+    def p_copy(i, k, t, relayed=False):
+        to = jnp.where(i < 4, r, other)
+        to = jnp.where(i == 0, other, (to + 2 * (i % 4)) % NR)
+        part = pl.ds(t * PART, PART)
         return pltpu.make_async_remote_copy(
-            src_ref=panel.at[:, at],
-            dst_ref=psbuf.at[k, :, pl.ds(t * PART, PART)],
+            src_ref=psbuf.at[k, :, part] if relayed else panel.at[:, p_rows(k, t)],
+            dst_ref=psbuf.at[k, :, part],
             send_sem=p_send.at[(t * 2 + k) * NR + i],
             recv_sem=p_recv.at[t * 2 + k],
-            device_id={"row": (r + i) % NR},
+            device_id={"row": to},
             device_id_type=MESH,
         )
 
+    def p_each(t, act):
+        @pl.when(is_root)
+        def _():
+            @pl.loop(0, 4)
+            def _(i):
+                for k in range(2):
+                    act(p_copy(i, k, t))
+
+            if t == SUB - 1:
+
+                @pl.loop(5, 8)
+                def _(i):
+                    for k in range(2):
+                        act(p_copy(i, k, t))
+
+    def p_relay(t, act):
+        @pl.loop(1, 4)
+        def _(i):
+            for k in range(2):
+                act(p_copy(i, k, t, True))
+
     def send_rows(t):
         from_sibling(LEAD + t * TURN)
+        p_each(t, lambda copy: copy.start())
 
         @pl.when(is_root)
         def _():
-            @pl.loop(1, NR)
-            def _(i):
+            for k in range(2):
+                psbuf[k, :, t * PART : (t + 1) * PART, :] = panel[:, p_rows(k, t), :]
+
+        if t > 0:
+
+            @pl.when(is_relay)
+            def _():
                 for k in range(2):
-                    p_copy(i, k, t).start()
-
-            for k in range(2):
-                at = pl.ds(pl.multiple_of(PANEL + t * SPAN + (x_hi + 2 * k) * PART, PART), PART)
-                psbuf[k, :, t * PART : (t + 1) * PART, :] = panel[:, at, :]
+                    p_copy(0, k, t - 1).wait_recv()
+                p_relay(t - 1, lambda copy: copy.start())
 
     forward_all(0, LEAD)
     phase(0)
-    forward_all(LEAD, LEAD + TURN // 2)
-    second(0)
-    forward_all(LEAD + TURN // 2, LEAD + TURN)
+    forward_all(LEAD, LEAD + TURN)
     phase(1)
     forward_all(LEAD + TURN, LEAD + TURN + TURN // 2)
-    second(1)
+    send_part(SUB)
     forward_all(LEAD + TURN + TURN // 2, AHEAD)
     for i in range(LEAD):
         from_sibling(i)
@@ -436,13 +468,11 @@
         def between(n):
             first = AHEAD + 8 * b + 2 * n
             forward_all(first, first + 2)
-            @pl.when((b == 0) & (n == 2))
-            def _():
-                second(2)
-
-            @pl.when((b == 1) & (n == 1))
-            def _():
-                second(3)
+            for t, point in enumerate((SEND_5, SEND_6, SEND_7)):
+
+                @pl.when(4 * b + n == point)
+                def _():
+                    send_part(SUB + 1 + t)
 
             for t in range(1, SUB):
                 due = LEAD + t * TURN + 4 * LAG - AHEAD - 1
@@ -464,9 +494,10 @@
     last = AHEAD + 32
     forward_all(last, last + 2)
 
-    @pl.when(jnp.logical_not(is_root))
-    def _():
-        for t in range(SUB):
+    for t in range(SUB):
+
+        @pl.when(jnp.logical_not(is_root | (is_relay & (t < SUB - 1))))
+        def _():
             for k in range(2):
                 p_copy(0, k, t).wait_recv()
 
@@ -488,11 +519,6 @@
 
     forward_all(last + 2, last + 3)
 
-    for t in range(SUB, 2 * SUB):
-        got_part(t)
-        assemble_here(t)
-
-    forward_all(last + 3, last + 4)
     drop = is_panel & (lax.broadcasted_iota(jnp.int32, (1, 2 * BLK), 1) < BLK)
 
     def out_copy(t, u):
@@ -524,21 +550,29 @@
                 acc[at, part, :] = (
                     jnp.where(drop, 0.0, acc[at, part, :]) - total[b * PART : (b + 1) * PART]
                 )
-            out_copy(t, u).start()
 
     update(0)
-    forward_all(last + 4, last + 5)
+    forward_all(last + 3, last + 5)
     update(1)
     forward_all(last + 5, STEPS)
     update(2)
     update(3)
 
     for t in range(SUB):
+        got_part(SUB + t)
+        assemble_here(SUB + t)
+
+        @pl.loop(0, KR // UNIT)
+        def _(u):
+            out_copy(t, u).start()
+
+    for t in range(SUB):
 
         @pl.loop(0, KR // UNIT)
         def _(u):
             out_copy(t, u).wait()
 
+        sent_part(t)
         sent_part(SUB + t)
 
     @pl.when(is_panel)
@@ -555,13 +589,13 @@
         def _(i):
             s_copy(i).wait_send()
 
-    @pl.when(is_root)
-    def _():
-        @pl.loop(1, NR)
-        def _(i):
-            for t in range(SUB):
-                for k in range(2):
-                    p_copy(i, k, t).wait_send()
+    for t in range(SUB):
+        p_each(t, lambda copy: copy.wait_send())
+        if t < SUB - 1:
+
+            @pl.when(is_relay)
+            def _():
+                p_relay(t, lambda copy: copy.wait_send())
 
     for g in range(2):
 

time: 220 us -> 205 us (0.932)
  Pallas kernels: 203 us -> 189 us
    pallas_call x1, Pallas kernels: 203 us -> 189 us  [local(): pl.pallas_call(kernel, out_shape=jax.ShapeDtypeStruct(held.shape, F32), i...]
where the time goes in v3:
time: 205 us; the launch traced here: 203 us
  Pallas kernels  189 us (92%)
  local copies, waits for them, and re-layouts  8.25 us (4%)
  other arithmetic  2.77 us (1%)
  between operations  2.67 us (1%)
    pallas_call x1, Pallas kernels, local(): pl.pallas_call(kernel, out_shape=jax.ShapeDtypeStruct(held.shape, F32), i...  189 us
    unnamed x2, local copies, waits for them, and re-layouts  5.62 us

profile of v3, /device:TPU:13, one launch (start us, length us, event | category | flops | bytes accessed | tf_op | source)
XLA Modules:
  0.0 203.1 jit_solution(15055043865162840057)
XLA Ops:
  0.0 0.1 add.89
  0.1 0.1 add.90
  0.2 0.8 reshape.112
  1.0 0.3 convert_reduce_fusion
  1.3 0.1 reduce_sum.40
  1.4 0.1 select_reduce_fusion.1
  1.5 0.1 select_reduce_fusion
  1.6 0.8 reshape.113
  2.3 0.1 slice_reduce_fusion
  2.5 0.1 reshape_squeeze.3
  2.5 0.6 dynamic_slice.12
  5.7 1.6 fusion
  7.3 0.1 copy.7
  7.4 0.1 add.94
  7.5 0.6 pad_add_fusion.tbl
  8.1 189.4 %shard_map.46 = f32[44,128,256]{2,1,0:T(8,128)} custom-call(s32[157]{0:T(256)} %pad_add_fusion.tbl, f32[44,128,256]{2,1,0:T(8,128)} %bitcast.9, f32[32,128,256]{2,1,0:T(8,128)} %bitcast.10), custom_call_target="tpu_custom_call" | custom-call | tf_op jit(solution)/shard_map/pallas_call | solution.py:648
  197.5 5.5 %copy.9 = f32[5632,256]{1,0:T(8,128)} copy(f32[5632,256]{1,0:T(8,128)} %bitcast.8) | data formatting | bytes 11534336
  (9 shorter events, 0.1 us)

commit v4 on v3

--- a/solution.py
+++ b/solution.py
@@ -21,9 +21,9 @@
 UNIT = 11
 WINDOW = 6
 LAG = 4
-SEND_5 = 3
-SEND_6 = 12
-SEND_7 = 14
+SEND_5 = 1
+SEND_6 = 5
+SEND_7 = 9
 STEPS = NCH + 4 * LAG
 AHEAD = LEAD + 2 * TURN
 HI = lax.Precision.HIGHEST
@@ -194,11 +194,6 @@
     for t in range(2 * SUB):
         ins[t][SLOTS] = jnp.zeros((PART, BLK), F32)
 
-    @pl.loop(0, SLOTS)
-    def _(slot):
-        block = children[tbl[slot]]
-        stage1[slot] = jnp.where(swap, block[:, :BLK], block[:, BLK:])
-
     @pl.when(jnp.logical_not(is_panel))
     def _():
         send_part(1)
@@ -246,6 +241,11 @@
         @pl.loop(1, NR)
         def _(i):
             s_copy(i).start()
+
+    @pl.loop(0, SLOTS)
+    def _(slot):
+        block = children[tbl[slot]]
+        stage1[slot] = jnp.where(swap, block[:, :BLK], block[:, BLK:])
 
     @pl.when(is_panel)
     def _():

time: 205 us -> 202 us (0.985)
  no operation moved by 1% of the time
where the time goes in v4:
time: 202 us
  Pallas kernels  188 us (93%)
  local copies, waits for them, and re-layouts  8.25 us (4%)
  other arithmetic  2.77 us (1%)
  between operations  2.67 us (1%)
    pallas_call x1, Pallas kernels, local(): pl.pallas_call(kernel, out_shape=jax.ShapeDtypeStruct(held.shape, F32), i...  188 us
    unnamed x2, local copies, waits for them, and re-layouts  5.62 us

profile of v4, /device:TPU:13, one launch (start us, length us, event | category | flops | bytes accessed | tf_op | source)
XLA Modules:
  0.0 201.7 jit_solution(10623985006469250690)
XLA Ops:
  0.0 0.1 add.89
  0.1 0.1 add.90
  0.2 0.8 reshape.112
  1.0 0.3 convert_reduce_fusion
  1.3 0.1 reduce_sum.40
  1.4 0.1 select_reduce_fusion.1
  1.5 0.1 select_reduce_fusion
  1.6 0.8 reshape.113
  2.3 0.1 slice_reduce_fusion
  2.5 0.1 reshape_squeeze.3
  2.5 0.6 dynamic_slice.12
  5.7 1.6 fusion
  7.3 0.1 copy.7
  7.4 0.1 add.94
  7.5 0.6 pad_add_fusion.tbl
  8.1 188.0 %shard_map.46 = f32[44,128,256]{2,1,0:T(8,128)} custom-call(s32[157]{0:T(256)} %pad_add_fusion.tbl, f32[44,128,256]{2,1,0:T(8,128)} %bitcast.9, f32[32,128,256]{2,1,0:T(8,128)} %bitcast.10), custom_call_target="tpu_custom_call" | custom-call | tf_op jit(solution)/shard_map/pallas_call | solution.py:648
  196.2 5.5 %copy.9 = f32[5632,256]{1,0:T(8,128)} copy(f32[5632,256]{1,0:T(8,128)} %bitcast.8) | data formatting | bytes 11534336
  (9 shorter events, 0.1 us)

commit v5 on v4

--- a/solution.py
+++ b/solution.py
@@ -21,9 +21,9 @@
 UNIT = 11
 WINDOW = 6
 LAG = 4
-SEND_5 = 1
-SEND_6 = 5
-SEND_7 = 9
+SEND_5 = 3
+SEND_6 = 7
+SEND_7 = 11
 STEPS = NCH + 4 * LAG
 AHEAD = LEAD + 2 * TURN
 HI = lax.Precision.HIGHEST
@@ -139,6 +139,17 @@
         def _(i):
             ex_copy(t, i).wait_send()
 
+    def send_later(t):
+        @pl.when(is_panel)
+        def _():
+            send_part(t)
+
+        if t + 1 < 2 * SUB:
+
+            @pl.when(jnp.logical_not(is_panel))
+            def _():
+                send_part(t + 1)
+
     def got_part(t):
         own_copy(t).wait()
 
@@ -197,6 +208,7 @@
     @pl.when(jnp.logical_not(is_panel))
     def _():
         send_part(1)
+        send_part(2)
 
     xmat[...] = jnp.zeros_like(xmat)
     load_front.wait()
@@ -357,7 +369,7 @@
 
     def phase(t):
         if t < 2:
-            send_part(t + 2)
+            send_later(t + 2)
         got_part(t)
 
         def store(k, total):
@@ -434,7 +446,7 @@
     forward_all(LEAD, LEAD + TURN)
     phase(1)
     forward_all(LEAD + TURN, LEAD + TURN + TURN // 2)
-    send_part(SUB)
+    send_later(SUB)
     forward_all(LEAD + TURN + TURN // 2, AHEAD)
     for i in range(LEAD):
         from_sibling(i)
@@ -472,7 +484,7 @@
 
                 @pl.when(4 * b + n == point)
                 def _():
-                    send_part(SUB + 1 + t)
+                    send_later(SUB + 1 + t)
 
             for t in range(1, SUB):
                 due = LEAD + t * TURN + 4 * LAG - AHEAD - 1

time: 202 us -> 198 us (0.980)
  Pallas kernels: 188 us -> 184 us
    pallas_call x1, Pallas kernels: 188 us -> 184 us  [local(): pl.pallas_call(kernel, out_shape=jax.ShapeDtypeStruct(held.shape, F32), i...]
where the time goes in v5:
time: 198 us; the launch traced here: 197 us
  Pallas kernels  184 us (93%)
  local copies, waits for them, and re-layouts  8.25 us (4%)
  other arithmetic  2.77 us (1%)
  between operations  2.67 us (1%)
    pallas_call x1, Pallas kernels, local(): pl.pallas_call(kernel, out_shape=jax.ShapeDtypeStruct(held.shape, F32), i...  184 us
    unnamed x2, local copies, waits for them, and re-layouts  5.62 us

profile of v5, /device:TPU:13, one launch (start us, length us, event | category | flops | bytes accessed | tf_op | source)
XLA Modules:
  0.0 197.5 jit_solution(18101273253838695645)
XLA Ops:
  0.0 0.1 add.89
  0.1 0.1 add.90
  0.2 0.8 reshape.112
  1.0 0.3 convert_reduce_fusion
  1.3 0.1 reduce_sum.40
  1.4 0.1 select_reduce_fusion.1
  1.5 0.1 select_reduce_fusion
  1.6 0.8 reshape.113
  2.3 0.1 slice_reduce_fusion
  2.5 0.1 reshape_squeeze.3
  2.5 0.6 dynamic_slice.12
  5.7 1.6 fusion
  7.3 0.1 copy.7
  7.4 0.1 add.94
  7.5 0.6 pad_add_fusion.tbl
  8.1 183.8 %shard_map.46 = f32[44,128,256]{2,1,0:T(8,128)} custom-call(s32[157]{0:T(256)} %pad_add_fusion.tbl, f32[44,128,256]{2,1,0:T(8,128)} %bitcast.9, f32[32,128,256]{2,1,0:T(8,128)} %bitcast.10), custom_call_target="tpu_custom_call" | custom-call | tf_op jit(solution)/shard_map/pallas_call | solution.py:660
  191.9 5.5 %copy.9 = f32[5632,256]{1,0:T(8,128)} copy(f32[5632,256]{1,0:T(8,128)} %bitcast.8) | data formatting | bytes 11534336
  (9 shorter events, 0.1 us)
